TPU v7x, 32 devices: a whole 2x2x4 slice. The times are simulated.
32 devices in a mesh: section: 8 (over z, y), fsdp: 4 (over x, core).
Axes of the slice: x: 2, y: 2, z: 4, core: 2. Of those that a mesh axis runs over, the one named last changes fastest.
Arguments:
- branch_in: bfloat16 [8, 8192, 128], P('section', 'fsdp'), may hold values from -0.0625 to 0.0625
- branch_out: bfloat16 [8, 128, 8192], P('section', None, 'fsdp'), may hold values from -0.5 to 0.5
- down_inputs: bfloat16 [8, 12, 32, 8192], P('section', None, 'fsdp'), may hold values from -6 to 6
- up_inputs: bfloat16 [8, 12, 32, 8192], P('section', None, 'fsdp'), may hold values from -6 to 6
- top_grads: bfloat16 [2, 12, 32, 8192], P(None, None, 'fsdp'), may hold values from -6 to 6
- plan: int32 [2, 12], replicated, may hold values from 0 to 11, each once within a row
- reward_pos: int32 [2, 12, 4], replicated, may hold values from 0 to 7
- reward_cot: float32 [2, 12, 4], replicated, may hold values from -4 to 4
- reward_head: float32 [8192], replicated, may hold values from -5 to 5
Outputs:
- grad_in: float32 [8, 8192, 128], P('section', 'fsdp')
- grad_out: float32 [8, 128, 8192], P('section', None, 'fsdp')
Inputs may be any that keep to these rules, and one draw needn't show every extreme that they name: Each row of plan names every microbatch once.
All inputs are finite; a program needn't handle non-finite values.
Results may differ from a plain program's by a relative error of at most 0.03.
Values may be sent and summed in bfloat16 or wider, within the bound.
A program may use at most 128 MiB of HBM per device.

v0:
```python
import jax
import jax.numpy as jnp
from jax import lax
from jax.sharding import PartitionSpec as P


def from_partner(value, axis, apart):
    mask = 2**apart
    pairs = [(source, source ^ mask) for source in range(lax.axis_size(axis))]
    return lax.ppermute(value, axis, pairs)


def passed_along(value, axis, steps):
    count = lax.axis_size(axis)
    initial, last = (max(0, -steps), min(count, count - steps))
    return lax.ppermute(value, axis, [(source, source + steps) for source in range(initial, last)])


def branch_grads(inputs, grad, w_in, w_out):
    pre_act = jnp.dot(inputs, w_in, preferred_element_type=jnp.float32)
    sig_val = jax.nn.sigmoid(pre_act)
    hidden = (pre_act * sig_val).astype(jnp.bfloat16)
    grad_hidden = lax.dot_general(
        grad, w_out, (((1,), (1,)), ((), ())), preferred_element_type=jnp.float32
    )
    grad_pre = (grad_hidden * sig_val * (1.0 + pre_act * (1.0 - sig_val))).astype(jnp.bfloat16)
    back_term = lax.dot_general(
        grad_pre, w_in, (((1,), (1,)), ((), ())), preferred_element_type=jnp.float32
    )
    back = (grad.astype(jnp.float32) + back_term).astype(jnp.bfloat16)
    return (hidden, grad_pre, back)


def bit_order(count):
    return list(range(count))


def fetch_mirror(packed):
    hops = lax.axis_size("section").bit_length() - 1
    for bit_index in bit_order(hops):
        packed = from_partner(packed, "section", bit_index)
    return packed


def send_mirror(packed):
    hops = lax.axis_size("section").bit_length() - 1
    for bit_index in bit_order(hops):
        packed = from_partner(packed.astype(jnp.bfloat16), "section", bit_index).astype(
            packed.dtype
        )
    return packed


def slot_pass(
    slot,
    starting,
    received,
    inputs,
    top,
    order,
    positions,
    rewards,
    head,
    row_global,
    seq_len,
    w_in,
    w_out,
    state,
):
    micro_count = inputs.shape[0]
    valid = jnp.logical_and(slot >= 0, slot < micro_count)
    clipped = jnp.clip(slot, 0, micro_count - 1)

    def active(operands):
        acc_in, acc_out = operands
        ident = lax.dynamic_index_in_dim(order, clipped, 0, keepdims=False)
        picked = jnp.arange(micro_count, dtype=jnp.int32) == ident
        pos_now = jnp.sum(jnp.where(picked[:, None], positions, 0), axis=0)
        cot_now = jnp.sum(jnp.where(picked[:, None], rewards, 0.0), axis=0)
        target = jnp.arange(positions.shape[1], dtype=jnp.int32) * seq_len + pos_now
        row_weight = jnp.sum(
            jnp.where(target[:, None] == row_global[None, :], cot_now[:, None], 0.0), axis=0
        )
        top_now = lax.dynamic_index_in_dim(top, clipped, 0, keepdims=False)
        first_grad = (top_now.astype(jnp.float32) + row_weight[:, None] * head[None, :]).astype(
            jnp.bfloat16
        )
        grad = jnp.where(starting, first_grad, received)
        rows_in = lax.dynamic_index_in_dim(inputs, ident, 0, keepdims=False)
        hidden, grad_pre, back = branch_grads(rows_in, grad, w_in, w_out)
        acc_in = acc_in + lax.dot_general(
            rows_in, grad_pre, (((0,), (0,)), ((), ())), preferred_element_type=jnp.float32
        )
        acc_out = acc_out + lax.dot_general(
            hidden, grad, (((0,), (0,)), ((), ())), preferred_element_type=jnp.float32
        )
        return ((acc_in, acc_out), back)

    def resting(operands):
        return (operands, jnp.zeros_like(received))

    return lax.cond(valid, active, resting, state)


def on_device(
    branch_in,
    branch_out,
    down_inputs,
    up_inputs,
    top_grads,
    plan,
    reward_pos,
    reward_cot,
    reward_head,
):
    section_count = lax.axis_size("section")
    section_idx = lax.axis_index("section")
    fsdp_count = lax.axis_size("fsdp")
    micro_count = down_inputs.shape[1]
    local_rows = down_inputs.shape[2]
    width = down_inputs.shape[3]
    seq_count = reward_pos.shape[2]
    seq_len = local_rows * fsdp_count // seq_count
    row_global = lax.axis_index("fsdp") * local_rows + jnp.arange(local_rows, dtype=jnp.int32)
    own_in_shard = branch_in[0]
    own_out_shard = branch_out[0]
    packed_own = jnp.stack([own_in_shard.reshape(own_out_shard.shape), own_out_shard])
    packed_far = fetch_mirror(packed_own)
    far_in_shard = packed_far[0].reshape(own_in_shard.shape)
    far_out_shard = packed_far[1]
    own_in, own_out = (
        lax.all_gather(own_in_shard, "fsdp", axis=0, tiled=True),
        lax.all_gather(own_out_shard, "fsdp", axis=1, tiled=True),
    )
    far_in, far_out = (
        lax.all_gather(far_in_shard, "fsdp", axis=0, tiled=True),
        lax.all_gather(far_out_shard, "fsdp", axis=1, tiled=True),
    )
    zero_in = jnp.zeros(own_in.shape, jnp.float32)
    zero_out = jnp.zeros(own_out.shape, jnp.float32)
    zero_rows = jnp.zeros((local_rows, width), jnp.bfloat16)
    down_state = (zero_in, zero_out)
    up_state = (zero_in, zero_out)

    def advance(step_idx, carry):
        recv_down, recv_up, state_down, state_up = carry
        slot_down = step_idx - (section_count - 1 - section_idx)
        slot_up = step_idx - section_idx
        state_down, back_down = slot_pass(
            slot_down,
            section_idx == section_count - 1,
            recv_down,
            down_inputs[0],
            top_grads[0],
            plan[0],
            reward_pos[0],
            reward_cot[0],
            reward_head,
            row_global,
            seq_len,
            own_in,
            own_out,
            state_down,
        )
        state_up, back_up = slot_pass(
            slot_up,
            section_idx == 0,
            recv_up,
            up_inputs[0],
            top_grads[1],
            plan[1],
            reward_pos[1],
            reward_cot[1],
            reward_head,
            row_global,
            seq_len,
            far_in,
            far_out,
            state_up,
        )
        recv_down = passed_along(back_down, "section", -1)
        recv_up = passed_along(back_up, "section", 1)
        return (recv_down, recv_up, state_down, state_up)

    carry = lax.fori_loop(
        0, section_count + micro_count - 1, advance, (zero_rows, zero_rows, down_state, up_state)
    )
    state_down = carry[2]
    state_up = carry[3]
    shares = (
        lax.psum_scatter(
            state_down[0].astype(jnp.bfloat16), "fsdp", scatter_dimension=0, tiled=True
        ).astype(jnp.float32),
        lax.psum_scatter(
            state_down[1].astype(jnp.bfloat16), "fsdp", scatter_dimension=1, tiled=True
        ).astype(jnp.float32),
        lax.psum_scatter(
            state_up[0].astype(jnp.bfloat16), "fsdp", scatter_dimension=0, tiled=True
        ).astype(jnp.float32),
        lax.psum_scatter(
            state_up[1].astype(jnp.bfloat16), "fsdp", scatter_dimension=1, tiled=True
        ).astype(jnp.float32),
    )
    packed_up = jnp.stack([shares[2].reshape(shares[3].shape), shares[3]])
    packed_back = send_mirror(packed_up)
    grad_in = shares[0] + packed_back[0].reshape(shares[0].shape)
    grad_out = shares[1] + packed_back[1]
    return (grad_in[None], grad_out[None])


def solution(mesh):
    in_specs = (
        P("section", "fsdp", None),
        P("section", None, "fsdp"),
        P("section", None, "fsdp", None),
        P("section", None, "fsdp", None),
        P(None, None, "fsdp", None),
        P(),
        P(),
        P(),
        P(),
    )
    out_specs = (P("section", "fsdp", None), P("section", None, "fsdp"))
    return jax.shard_map(
        on_device, mesh=mesh, in_specs=in_specs, out_specs=out_specs, check_vma=False
    )
```

profile of v0, /device:TPU:8, one launch (start us, length us, event | category | flops | bytes accessed | tf_op | source)
XLA Modules:
  0.0 1057.6 jit_solution(13741040965211246680)
XLA Ops:
  12.0 23.3 %collective-permute-done.2 = bf16[2,128,2048]{2,1,0:T(8,128)(2,1)S(1)} collective-permute-done((bf16[2,128,2048]{2,1,0:T(8,128)(2,1)S(1)}, bf16[2,128,2048]{2,1,0:T(8,128)(2,1)S(1)}, u32[]{:S(2)}, u32[]{:S(2)}) %collective-permute-start.2) | collective-permute-done | bytes 1048608 | tf_op jit(solution)/shard_map/ppermute | solution.py:10
  35.6 23.8 %collective-permute-done.3 = bf16[2,128,2048]{2,1,0:T(8,128)(2,1)S(1)} collective-permute-done((bf16[2,128,2048]{2,1,0:T(8,128)(2,1)S(1)}, bf16[2,128,2048]{2,1,0:T(8,128)(2,1)S(1)}, u32[]{:S(2)}, u32[]{:S(2)}) %collective-permute-start.3) | collective-permute-done | bytes 1048608 | tf_op jit(solution)/shard_map/ppermute | solution.py:10
  61.9 43.0 %collective-permute-done.4 = bf16[2,128,2048]{2,1,0:T(8,128)(2,1)S(1)} collective-permute-done((bf16[2,128,2048]{2,1,0:T(8,128)(2,1)S(1)}, bf16[2,128,2048]{2,1,0:T(8,128)(2,1)S(1)}, u32[]{:S(2)}, u32[]{:S(2)}) %collective-permute-start.4) | collective-permute-done | bytes 1048608 | tf_op jit(solution)/shard_map/ppermute | solution.py:10
  107.5 24.0 %all-gather.8.cloned.1.call-done = bf16[8192,128]{1,0:T(8,128)(2,1)} async-done(((bf16[2048,128]{1,0:T(8,128)(2,1)}), bf16[8192,128]{1,0:T(8,128)(2,1)}) %all-gather.8.cloned.1.call-update) | async-done | bytes 2097168 | tf_op jit(solution)/shard_map/all_gather | solution.py:136
  131.6 24.6 %all-gather.14.cloned.1.call-done = bf16[1,128,8192]{2,1,0:T(8,128)(2,1)} async-done(((bf16[1,128,2048]{2,1,0:T(8,128)(2,1)}), bf16[1,128,8192]{2,1,0:T(8,128)(2,1)}) %all-gather.14.cloned.1.call-update) | async-done | bytes 2097168 | tf_op jit(solution)/shard_map/all_gather | solution.py:137
  165.7 684.3 %while.25 = (s32[]{:T(128)}, bf16[8,8192]{1,0:T(8,128)(2,1)S(1)}, bf16[8,8192]{1,0:T(8,128)(2,1)S(1)}, f32[8192,128]{1,0:T(8,128)}, f32[128,8192]{1,0:T(8,128)},...) while((s32[]{:T(128)}, bf16[8,8192]{1,0:T(8,128)(2,1)S(1)}, ...), condition=%wide.region_11.12_spmd.clone, body=%wide.region_0.11_spmd.clone.sunk | while | flops 173044320 | bytes 206936608 | solution.py:185
  196.5 20.3 %collective-permute-done.1 = bf16[8,8192]{1,0:T(8,128)(2,1)S(1)} collective-permute-done((bf16[8,8192]{1,0:T(8,128)(2,1)S(1)}, bf16[8,8192]{1,0:T(8,128)(2,1)S(1)}, u32[]{:S(2)}, u32[]{:S(2)}) %collective-permute-start.1) | collective-permute-done | bytes 131104 | tf_op jit(solution)/shard_map/while/body/eval_jaxpr/ppermute | solution.py:16
  220.5 17.7 %conditional.7 = (f32[8192,128]{1,0:T(8,128)}, f32[128,8192]{1,0:T(8,128)}, bf16[8,8192]{1,0:T(8,128)(2,1)S(1)}) conditional(s32[]{:T(128)} %convert_element_type.118, (f32[8192,128]{1,0:T(8,128)}, f32[128,8192]{1,0:T(8,128)}) %tuple.66, (s32[2,12]{1,0:T(2,128)S(1)}, s32[]{:T(128)}, bf16[1,12,8,8192]{3,2,1,0:T(8,128)(2,1)}, pred[]{:T(512)}, ...), branch_computations={%region_6.6_spmd, %region_7.10_spmd} | conditional | flops 86522152 | bytes 102943680 | solution.py:102
  247.9 17.7 %conditional.7 = (f32[8192,128]{1,0:T(8,128)}, f32[128,8192]{1,0:T(8,128)}, bf16[8,8192]{1,0:T(8,128)(2,1)S(1)}) conditional(s32[]{:T(128)} %convert_element_type.118, (f32[8192,128]{1,0:T(8,128)}, f32[128,8192]{1,0:T(8,128)}) %tuple.66, (s32[2,12]{1,0:T(2,128)S(1)}, s32[]{:T(128)}, bf16[1,12,8,8192]{3,2,1,0:T(8,128)(2,1)}, pred[]{:T(512)}, ...), branch_computations={%region_6.6_spmd, %region_7.10_spmd} | conditional | flops 86522152 | bytes 102943680 | solution.py:102
  275.3 17.7 %conditional.7 = (f32[8192,128]{1,0:T(8,128)}, f32[128,8192]{1,0:T(8,128)}, bf16[8,8192]{1,0:T(8,128)(2,1)S(1)}) conditional(s32[]{:T(128)} %convert_element_type.118, (f32[8192,128]{1,0:T(8,128)}, f32[128,8192]{1,0:T(8,128)}) %tuple.66, (s32[2,12]{1,0:T(2,128)S(1)}, s32[]{:T(128)}, bf16[1,12,8,8192]{3,2,1,0:T(8,128)(2,1)}, pred[]{:T(512)}, ...), branch_computations={%region_6.6_spmd, %region_7.10_spmd} | conditional | flops 86522152 | bytes 102943680 | solution.py:102
  293.0 19.2 %collective-permute-start.1 = (bf16[8,8192]{1,0:T(8,128)(2,1)S(1)}, bf16[8,8192]{1,0:T(8,128)(2,1)S(1)}, u32[]{:S(2)}, u32[]{:S(2)}) collective-permute-start(bf16[8,8192]{1,0:T(8,128)(2,1)S(1)} %get-tuple-element.808), channel_id=1, source_target_pairs={{0,4},{4,8},{8,12},{12,16},{16,20},{20,24},{24,28},{1,5},{5,9},{9,... | collective-permute-start | bytes 393224 | tf_op jit(solution)/shard_map/while/body/eval_jaxpr/ppermute | solution.py:16
  332.9 17.7 %conditional.7 = (f32[8192,128]{1,0:T(8,128)}, f32[128,8192]{1,0:T(8,128)}, bf16[8,8192]{1,0:T(8,128)(2,1)S(1)}) conditional(s32[]{:T(128)} %convert_element_type.118, (f32[8192,128]{1,0:T(8,128)}, f32[128,8192]{1,0:T(8,128)}) %tuple.66, (s32[2,12]{1,0:T(2,128)S(1)}, s32[]{:T(128)}, bf16[1,12,8,8192]{3,2,1,0:T(8,128)(2,1)}, pred[]{:T(512)}, ...), branch_computations={%region_6.6_spmd, %region_7.10_spmd} | conditional | flops 86522152 | bytes 102943680 | solution.py:102
  376.4 17.7 %conditional.7 = (f32[8192,128]{1,0:T(8,128)}, f32[128,8192]{1,0:T(8,128)}, bf16[8,8192]{1,0:T(8,128)(2,1)S(1)}) conditional(s32[]{:T(128)} %convert_element_type.118, (f32[8192,128]{1,0:T(8,128)}, f32[128,8192]{1,0:T(8,128)}) %tuple.66, (s32[2,12]{1,0:T(2,128)S(1)}, s32[]{:T(128)}, bf16[1,12,8,8192]{3,2,1,0:T(8,128)(2,1)}, pred[]{:T(512)}, ...), branch_computations={%region_6.6_spmd, %region_7.10_spmd} | conditional | flops 86522152 | bytes 102943680 | solution.py:102
  420.0 17.7 %conditional.7 = (f32[8192,128]{1,0:T(8,128)}, f32[128,8192]{1,0:T(8,128)}, bf16[8,8192]{1,0:T(8,128)(2,1)S(1)}) conditional(s32[]{:T(128)} %convert_element_type.118, (f32[8192,128]{1,0:T(8,128)}, f32[128,8192]{1,0:T(8,128)}) %tuple.66, (s32[2,12]{1,0:T(2,128)S(1)}, s32[]{:T(128)}, bf16[1,12,8,8192]{3,2,1,0:T(8,128)(2,1)}, pred[]{:T(512)}, ...), branch_computations={%region_6.6_spmd, %region_7.10_spmd} | conditional | flops 86522152 | bytes 102943680 | solution.py:102
  550.8 17.7 %conditional.7 = (f32[8192,128]{1,0:T(8,128)}, f32[128,8192]{1,0:T(8,128)}, bf16[8,8192]{1,0:T(8,128)(2,1)S(1)}) conditional(s32[]{:T(128)} %convert_element_type.118, (f32[8192,128]{1,0:T(8,128)}, f32[128,8192]{1,0:T(8,128)}) %tuple.66, (s32[2,12]{1,0:T(2,128)S(1)}, s32[]{:T(128)}, bf16[1,12,8,8192]{3,2,1,0:T(8,128)(2,1)}, pred[]{:T(512)}, ...), branch_computations={%region_6.6_spmd, %region_7.10_spmd} | conditional | flops 86522152 | bytes 102943680 | solution.py:102
  594.4 17.7 %conditional.7 = (f32[8192,128]{1,0:T(8,128)}, f32[128,8192]{1,0:T(8,128)}, bf16[8,8192]{1,0:T(8,128)(2,1)S(1)}) conditional(s32[]{:T(128)} %convert_element_type.118, (f32[8192,128]{1,0:T(8,128)}, f32[128,8192]{1,0:T(8,128)}) %tuple.66, (s32[2,12]{1,0:T(2,128)S(1)}, s32[]{:T(128)}, bf16[1,12,8,8192]{3,2,1,0:T(8,128)(2,1)}, pred[]{:T(512)}, ...), branch_computations={%region_6.6_spmd, %region_7.10_spmd} | conditional | flops 86522152 | bytes 102943680 | solution.py:102
  637.9 17.7 %conditional.7 = (f32[8192,128]{1,0:T(8,128)}, f32[128,8192]{1,0:T(8,128)}, bf16[8,8192]{1,0:T(8,128)(2,1)S(1)}) conditional(s32[]{:T(128)} %convert_element_type.118, (f32[8192,128]{1,0:T(8,128)}, f32[128,8192]{1,0:T(8,128)}) %tuple.66, (s32[2,12]{1,0:T(2,128)S(1)}, s32[]{:T(128)}, bf16[1,12,8,8192]{3,2,1,0:T(8,128)(2,1)}, pred[]{:T(512)}, ...), branch_computations={%region_6.6_spmd, %region_7.10_spmd} | conditional | flops 86522152 | bytes 102943680 | solution.py:102
  681.5 17.7 %conditional.7 = (f32[8192,128]{1,0:T(8,128)}, f32[128,8192]{1,0:T(8,128)}, bf16[8,8192]{1,0:T(8,128)(2,1)S(1)}) conditional(s32[]{:T(128)} %convert_element_type.118, (f32[8192,128]{1,0:T(8,128)}, f32[128,8192]{1,0:T(8,128)}) %tuple.66, (s32[2,12]{1,0:T(2,128)S(1)}, s32[]{:T(128)}, bf16[1,12,8,8192]{3,2,1,0:T(8,128)(2,1)}, pred[]{:T(512)}, ...), branch_computations={%region_6.6_spmd, %region_7.10_spmd} | conditional | flops 86522152 | bytes 102943680 | solution.py:102
  725.2 22.4 %collective-permute-start.1 = (bf16[8,8192]{1,0:T(8,128)(2,1)S(1)}, bf16[8,8192]{1,0:T(8,128)(2,1)S(1)}, u32[]{:S(2)}, u32[]{:S(2)}) collective-permute-start(bf16[8,8192]{1,0:T(8,128)(2,1)S(1)} %get-tuple-element.808), channel_id=1, source_target_pairs={{0,4},{4,8},{8,12},{12,16},{16,20},{20,24},{24,28},{1,5},{5,9},{9,... | collective-permute-start | bytes 393224 | tf_op jit(solution)/shard_map/while/body/eval_jaxpr/ppermute | solution.py:16
  865.3 49.9 %reduce-scatter.7.cloned.1.call-done = bf16[2048,128]{1,0:T(8,128)(2,1)} async-done(((bf16[8192,128]{1,0:T(8,128)(2,1)}), bf16[2048,128]{1,0:T(8,128)(2,1)}) %reduce-scatter.7.cloned.1.call-update) | async-done | bytes 524304 | tf_op jit(solution)/shard_map/reduce_scatter | solution.py:197
  916.4 32.7 %reduce-scatter.9.cloned.1.call-done = bf16[128,2048]{1,0:T(8,128)(2,1)} async-done(((bf16[128,8192]{1,0:T(8,128)(2,1)}), bf16[128,2048]{1,0:T(8,128)(2,1)}) %reduce-scatter.9.cloned.1.call-update) | async-done | bytes 524304 | tf_op jit(solution)/shard_map/reduce_scatter | solution.py:200
  951.9 23.4 %collective-permute-done.5 = bf16[2,128,2048]{2,1,0:T(8,128)(2,1)S(1)} collective-permute-done((bf16[2,128,2048]{2,1,0:T(8,128)(2,1)S(1)}, bf16[2,128,2048]{2,1,0:T(8,128)(2,1)S(1)}, u32[]{:S(2)}, u32[]{:S(2)}) %collective-permute-start.5) | collective-permute-done | bytes 1048608 | tf_op jit(solution)/shard_map/ppermute | solution.py:10
  975.8 23.6 %collective-permute-done.6 = bf16[2,128,2048]{2,1,0:T(8,128)(2,1)S(1)} collective-permute-done((bf16[2,128,2048]{2,1,0:T(8,128)(2,1)S(1)}, bf16[2,128,2048]{2,1,0:T(8,128)(2,1)S(1)}, u32[]{:S(2)}, u32[]{:S(2)}) %collective-permute-start.6) | collective-permute-done | bytes 1048608 | tf_op jit(solution)/shard_map/ppermute | solution.py:10
  1001.8 43.2 %collective-permute-done.7 = bf16[2,128,2048]{2,1,0:T(8,128)(2,1)S(1)} collective-permute-done((bf16[2,128,2048]{2,1,0:T(8,128)(2,1)S(1)}, bf16[2,128,2048]{2,1,0:T(8,128)(2,1)S(1)}, u32[]{:S(2)}, u32[]{:S(2)}) %collective-permute-start.7) | collective-permute-done | bytes 1048608 | tf_op jit(solution)/shard_map/ppermute | solution.py:10
  (769 shorter events, 852.7 us)
Async XLA Ops:
  7.2 100.4 %all-gather.12.cloned.1.call-start = ((), (), s32[]{:S(2)}) async-start(), calls=%async_computation.10 | async-start | bytes 2621440 | tf_op jit(solution)/shard_map/all_gather | solution.py:132
  7.9 99.6 %all-gather.10.cloned.1.call-start = ((), (), s32[]{:S(2)}) async-start(), calls=%async_computation.9 | async-start | bytes 2621440 | tf_op jit(solution)/shard_map/all_gather | solution.py:133
  10.4 25.0 %collective-permute-start.2 = (bf16[2,128,2048]{2,1,0:T(8,128)(2,1)S(1)}, bf16[2,128,2048]{2,1,0:T(8,128)(2,1)S(1)}, u32[]{:S(2)}, u32[]{:S(2)}) collective-permute-start(bf16[2,128,2048]{2,1,0:T(8,128)(2,1)S(1)} %pad_maximum_fusion), channel_id=1, source_target_pairs={{0,4},{4,0},{8,12},{12,8},{16,20},{20,16},{24,28},{28,24},{1,5},{5... | collective-permute-start | bytes 3145736 | tf_op jit(solution)/shard_map/ppermute | solution.py:10
  12.0 119.6 %all-gather.8.cloned.1.call-start = ((), (), s32[]{:S(2)}) async-start(), calls=%async_computation.4 | async-start | bytes 2621440 | tf_op jit(solution)/shard_map/all_gather | solution.py:136
  59.3 45.6 %collective-permute-start.4 = (bf16[2,128,2048]{2,1,0:T(8,128)(2,1)S(1)}, bf16[2,128,2048]{2,1,0:T(8,128)(2,1)S(1)}, u32[]{:S(2)}, u32[]{:S(2)}) collective-permute-start(bf16[2,128,2048]{2,1,0:T(8,128)(2,1)S(1)} %collective-permute-done.3), channel_id=1, source_target_pairs={{0,16},{4,20},{8,24},{12,28},{16,0},{20,4},{24,8},{28,12},{1,17},{... | collective-permute-start | bytes 3145736 | tf_op jit(solution)/shard_map/ppermute | solution.py:10
  106.9 49.3 %all-gather.14.cloned.1.call-start = ((), (), s32[]{:S(2)}) async-start(), calls=%async_computation.11 | async-start | bytes 2621440 | tf_op jit(solution)/shard_map/all_gather | solution.py:137
  107.4 807.7 %reduce-scatter.7.cloned.1.call-start = ((), (), s32[]{:S(2)}) async-start(), calls=%async_computation.6 | async-start | bytes 2621440 | tf_op jit(solution)/shard_map/reduce_scatter | solution.py:197
  273.4 38.8 %collective-permute-start = (bf16[8,8192]{1,0:T(8,128)(2,1)S(1)}, bf16[8,8192]{1,0:T(8,128)(2,1)S(1)}, u32[]{:S(2)}, u32[]{:S(2)}) collective-permute-start(bf16[8,8192]{1,0:T(8,128)(2,1)S(1)} %get-tuple-element.807), channel_id=1, source_target_pairs={{4,0},{8,4},{12,8},{16,12},{20,16},{24,20},{28,24},{5,1},{9,5},{13... | collective-permute-start | bytes 393224 | tf_op jit(solution)/shard_map/while/body/eval_jaxpr/ppermute | solution.py:16
  330.9 24.4 %collective-permute-start = (bf16[8,8192]{1,0:T(8,128)(2,1)S(1)}, bf16[8,8192]{1,0:T(8,128)(2,1)S(1)}, u32[]{:S(2)}, u32[]{:S(2)}) collective-permute-start(bf16[8,8192]{1,0:T(8,128)(2,1)S(1)} %get-tuple-element.807), channel_id=1, source_target_pairs={{4,0},{8,4},{12,8},{16,12},{20,16},{24,20},{28,24},{5,1},{9,5},{13... | collective-permute-start | bytes 393224 | tf_op jit(solution)/shard_map/while/body/eval_jaxpr/ppermute | solution.py:16
  374.5 24.4 %collective-permute-start = (bf16[8,8192]{1,0:T(8,128)(2,1)S(1)}, bf16[8,8192]{1,0:T(8,128)(2,1)S(1)}, u32[]{:S(2)}, u32[]{:S(2)}) collective-permute-start(bf16[8,8192]{1,0:T(8,128)(2,1)S(1)} %get-tuple-element.807), channel_id=1, source_target_pairs={{4,0},{8,4},{12,8},{16,12},{20,16},{24,20},{28,24},{5,1},{9,5},{13... | collective-permute-start | bytes 393224 | tf_op jit(solution)/shard_map/while/body/eval_jaxpr/ppermute | solution.py:16
  418.1 24.4 %collective-permute-start = (bf16[8,8192]{1,0:T(8,128)(2,1)S(1)}, bf16[8,8192]{1,0:T(8,128)(2,1)S(1)}, u32[]{:S(2)}, u32[]{:S(2)}) collective-permute-start(bf16[8,8192]{1,0:T(8,128)(2,1)S(1)} %get-tuple-element.807), channel_id=1, source_target_pairs={{4,0},{8,4},{12,8},{16,12},{20,16},{24,20},{28,24},{5,1},{9,5},{13... | collective-permute-start | bytes 393224 | tf_op jit(solution)/shard_map/while/body/eval_jaxpr/ppermute | solution.py:16
  461.7 24.4 %collective-permute-start = (bf16[8,8192]{1,0:T(8,128)(2,1)S(1)}, bf16[8,8192]{1,0:T(8,128)(2,1)S(1)}, u32[]{:S(2)}, u32[]{:S(2)}) collective-permute-start(bf16[8,8192]{1,0:T(8,128)(2,1)S(1)} %get-tuple-element.807), channel_id=1, source_target_pairs={{4,0},{8,4},{12,8},{16,12},{20,16},{24,20},{28,24},{5,1},{9,5},{13... | collective-permute-start | bytes 393224 | tf_op jit(solution)/shard_map/while/body/eval_jaxpr/ppermute | solution.py:16
  505.3 24.4 %collective-permute-start = (bf16[8,8192]{1,0:T(8,128)(2,1)S(1)}, bf16[8,8192]{1,0:T(8,128)(2,1)S(1)}, u32[]{:S(2)}, u32[]{:S(2)}) collective-permute-start(bf16[8,8192]{1,0:T(8,128)(2,1)S(1)} %get-tuple-element.807), channel_id=1, source_target_pairs={{4,0},{8,4},{12,8},{16,12},{20,16},{24,20},{28,24},{5,1},{9,5},{13... | collective-permute-start | bytes 393224 | tf_op jit(solution)/shard_map/while/body/eval_jaxpr/ppermute | solution.py:16
  548.8 24.4 %collective-permute-start = (bf16[8,8192]{1,0:T(8,128)(2,1)S(1)}, bf16[8,8192]{1,0:T(8,128)(2,1)S(1)}, u32[]{:S(2)}, u32[]{:S(2)}) collective-permute-start(bf16[8,8192]{1,0:T(8,128)(2,1)S(1)} %get-tuple-element.807), channel_id=1, source_target_pairs={{4,0},{8,4},{12,8},{16,12},{20,16},{24,20},{28,24},{5,1},{9,5},{13... | collective-permute-start | bytes 393224 | tf_op jit(solution)/shard_map/while/body/eval_jaxpr/ppermute | solution.py:16
  592.4 24.4 %collective-permute-start = (bf16[8,8192]{1,0:T(8,128)(2,1)S(1)}, bf16[8,8192]{1,0:T(8,128)(2,1)S(1)}, u32[]{:S(2)}, u32[]{:S(2)}) collective-permute-start(bf16[8,8192]{1,0:T(8,128)(2,1)S(1)} %get-tuple-element.807), channel_id=1, source_target_pairs={{4,0},{8,4},{12,8},{16,12},{20,16},{24,20},{28,24},{5,1},{9,5},{13... | collective-permute-start | bytes 393224 | tf_op jit(solution)/shard_map/while/body/eval_jaxpr/ppermute | solution.py:16
  636.0 24.4 %collective-permute-start = (bf16[8,8192]{1,0:T(8,128)(2,1)S(1)}, bf16[8,8192]{1,0:T(8,128)(2,1)S(1)}, u32[]{:S(2)}, u32[]{:S(2)}) collective-permute-start(bf16[8,8192]{1,0:T(8,128)(2,1)S(1)} %get-tuple-element.807), channel_id=1, source_target_pairs={{4,0},{8,4},{12,8},{16,12},{20,16},{24,20},{28,24},{5,1},{9,5},{13... | collective-permute-start | bytes 393224 | tf_op jit(solution)/shard_map/while/body/eval_jaxpr/ppermute | solution.py:16
  679.6 24.4 %collective-permute-start = (bf16[8,8192]{1,0:T(8,128)(2,1)S(1)}, bf16[8,8192]{1,0:T(8,128)(2,1)S(1)}, u32[]{:S(2)}, u32[]{:S(2)}) collective-permute-start(bf16[8,8192]{1,0:T(8,128)(2,1)S(1)} %get-tuple-element.807), channel_id=1, source_target_pairs={{4,0},{8,4},{12,8},{16,12},{20,16},{24,20},{28,24},{5,1},{9,5},{13... | collective-permute-start | bytes 393224 | tf_op jit(solution)/shard_map/while/body/eval_jaxpr/ppermute | solution.py:16
  723.2 24.4 %collective-permute-start = (bf16[8,8192]{1,0:T(8,128)(2,1)S(1)}, bf16[8,8192]{1,0:T(8,128)(2,1)S(1)}, u32[]{:S(2)}, u32[]{:S(2)}) collective-permute-start(bf16[8,8192]{1,0:T(8,128)(2,1)S(1)} %get-tuple-element.807), channel_id=1, source_target_pairs={{4,0},{8,4},{12,8},{16,12},{20,16},{24,20},{28,24},{5,1},{9,5},{13... | collective-permute-start | bytes 393224 | tf_op jit(solution)/shard_map/while/body/eval_jaxpr/ppermute | solution.py:16
  725.2 24.9 %collective-permute-start.1 = (bf16[8,8192]{1,0:T(8,128)(2,1)S(1)}, bf16[8,8192]{1,0:T(8,128)(2,1)S(1)}, u32[]{:S(2)}, u32[]{:S(2)}) collective-permute-start(bf16[8,8192]{1,0:T(8,128)(2,1)S(1)} %get-tuple-element.808), channel_id=1, source_target_pairs={{0,4},{4,8},{8,12},{12,16},{16,20},{20,24},{24,28},{1,5},{5,9},{9,... | collective-permute-start | bytes 393224 | tf_op jit(solution)/shard_map/while/body/eval_jaxpr/ppermute | solution.py:16
  853.7 95.5 %reduce-scatter.9.cloned.1.call-start = ((), (), s32[]{:S(2)}) async-start(), calls=%async_computation.7 | async-start | bytes 2621440 | tf_op jit(solution)/shard_map/reduce_scatter | solution.py:200
  857.6 188.9 %reduce-scatter.11.cloned.1.call-start = ((), (), s32[]{:S(2)}) async-start(), calls=%async_computation.8 | async-start | bytes 2621440 | tf_op jit(solution)/shard_map/reduce_scatter | solution.py:194
  861.5 187.3 %reduce-scatter.5.cloned.1.call-start = ((), (), s32[]{:S(2)}) async-start(), calls=%async_computation.5 | async-start | bytes 2621440 | tf_op jit(solution)/shard_map/reduce_scatter | solution.py:191
  950.3 25.0 %collective-permute-start.5 = (bf16[2,128,2048]{2,1,0:T(8,128)(2,1)S(1)}, bf16[2,128,2048]{2,1,0:T(8,128)(2,1)S(1)}, u32[]{:S(2)}, u32[]{:S(2)}) collective-permute-start(bf16[2,128,2048]{2,1,0:T(8,128)(2,1)S(1)} %pad_maximum_fusion.1), channel_id=1, source_target_pairs={{0,4},{4,0},{8,12},{12,8},{16,20},{20,16},{24,28},{28,24},{1,5},{5... | collective-permute-start | bytes 3145736 | tf_op jit(solution)/shard_map/ppermute | solution.py:10
  999.4 45.6 %collective-permute-start.7 = (bf16[2,128,2048]{2,1,0:T(8,128)(2,1)S(1)}, bf16[2,128,2048]{2,1,0:T(8,128)(2,1)S(1)}, u32[]{:S(2)}, u32[]{:S(2)}) collective-permute-start(bf16[2,128,2048]{2,1,0:T(8,128)(2,1)S(1)} %collective-permute-done.6), channel_id=1, source_target_pairs={{0,16},{4,20},{8,24},{12,28},{16,0},{20,4},{24,8},{28,12},{1,17},{... | collective-permute-start | bytes 3145736 | tf_op jit(solution)/shard_map/ppermute | solution.py:10
  (154 other events, 702.3 us)
Sparse Core Ops, SparseCore 0:
  9.6 23.7 all-gather.11
  34.9 22.5 all-gather.9
  107.0 24.5 all-gather.7
  133.5 22.5 all-gather.13
  853.8 61.3 reduce-scatter.6
  917.7 31.3 reduce-scatter.8
  951.7 31.4 reduce-scatter.10
  985.8 31.3 reduce-scatter.4
where the time goes:
time: 1060 us
  waiting for transfers between devices  406 us (38%)
  matrix products  199 us (19%)
  starting transfers between devices  192 us (18%)
  local copies, waits for them, and re-layouts  151 us (14%)
  loops' own time  47.9 us (5%)
  other arithmetic  47.8 us (5%)
  between operations  14.2 us (1%)
    ppermute x38, starting transfers between devices, passed_along(): lax.ppermute(value, axis, [(source, source + steps) for source in range(i...  183 us
    ppermute x6, waiting for transfers between devices, from_partner(): return lax.ppermute(value, axis, pairs)  180 us
    ppermute x38, waiting for transfers between devices, passed_along(): lax.ppermute(value, axis, [(source, source + steps) for source in range(i...  92.9 us
    cond x240, local copies, waits for them, and re-layouts  81.4 us
    dot_general x24, matrix products, active(): lax.dot_general(rows_in, grad_pre, (((0,), (0,)), ((), ())), preferred_el...  73.4 us
    reduce_scatter x1, waiting for transfers between devices, on_device(): lax.psum_scatter(state_up[0].astype(jnp.bfloat16), 'fsdp', scatter_dimens...  49.9 us
    another operation x38, loops' own time, slot_pass(): return lax.cond(valid, active, resting, state)  47.1 us
    dot_general x24, matrix products, branch_grads(): pre_act = jnp.dot(inputs, w_in, preferred_element_type=jnp.float32)  41.7 us
  transfers between devices with their start and end apart: 52, of which 35 were waited for; matrix products, arithmetic and copies ran while one was open for 17% of the time, Pallas kernels for 0%

commit v1 on v0

v1 whole, which is shorter than its diff:
```python
import jax
import jax.numpy as jnp
from jax import lax
from jax.sharding import PartitionSpec as P

BF = jnp.bfloat16
F32 = jnp.float32


def dot(a, b, ca, cb):
    return lax.dot_general(a, b, (((ca,), (cb,)), ((), ())), preferred_element_type=F32)


def on_device(
    branch_in,
    branch_out,
    down_inputs,
    up_inputs,
    top_grads,
    plan,
    reward_pos,
    reward_cot,
    reward_head,
):
    S = lax.axis_size("section")
    k = lax.axis_index("section")
    F = lax.axis_size("fsdp")
    f = lax.axis_index("fsdp")
    _, micro, r, D = down_inputs.shape
    n = micro * r
    seqs = reward_pos.shape[2]
    seq_len = r * F // seqs
    w_in, w_out = branch_in[0], branch_out[0]
    R = w_in.shape[1]

    x = jnp.stack([down_inputs[0].reshape(n, D), up_inputs[0].reshape(n, D)])
    xs = lax.all_to_all(x, "fsdp", split_axis=2, concat_axis=1, tiled=True)
    w_all = lax.all_gather(w_in, "section", axis=0, tiled=False)

    row_global = f * r + jnp.arange(r, dtype=jnp.int32)
    pick = plan[:, :, None] == jnp.arange(micro, dtype=jnp.int32)
    reward_pos = jnp.sum(jnp.where(pick[..., None], reward_pos[:, None], 0), axis=2)
    reward_cot = jnp.sum(jnp.where(pick[..., None], reward_cot[:, None], 0.0), axis=2)
    order = jnp.einsum(
        "djm,rs->djrms", pick.astype(BF), jnp.eye(r, dtype=BF), preferred_element_type=F32
    )
    order = order.astype(BF).reshape(2, n, n)
    target = jnp.arange(seqs, dtype=jnp.int32) * seq_len + reward_pos
    weight = jnp.sum(
        jnp.where(target[..., None] == row_global, reward_cot[..., None], 0.0), axis=2
    )
    first = (top_grads.astype(F32) + weight[..., None] * reward_head).astype(BF)
    gs = lax.all_to_all(
        first.reshape(2, n, D), "fsdp", split_axis=2, concat_axis=1, tiled=True
    )
    N = n * F

    w_far = lax.dynamic_index_in_dim(w_all, S - 1 - k, 0, keepdims=False)
    pre = [dot(xs[0], w_in, 1, 0), dot(xs[1], w_far, 1, 0)]
    top = dot(gs.reshape(2 * N, -1), w_out, 1, 1).reshape(2, N, R)
    parts = jnp.stack([pre[0], pre[1], top[0], top[1]]).astype(BF)
    mix = lax.dot_general(
        w_all, w_out, (((1,), (1,)), ((), ())), preferred_element_type=F32
    ).astype(BF)
    parts = lax.psum_scatter(parts, "fsdp", scatter_dimension=1, tiled=True)
    mix = lax.psum_scatter(mix, "fsdp", scatter_dimension=1, tiled=True)
    parts = lax.all_gather(parts, "section", axis=0)
    mix = lax.all_gather(mix, ("section", "fsdp"), axis=0)
    mix = mix.reshape(S, F, S, R // F, R).transpose(0, 2, 1, 3, 4).reshape(S, S, R, R)

    pres = jnp.einsum("dij,ldjr->ldir", order, parts[:, :2], preferred_element_type=F32)

    grads = [None] * S
    hiddens = [None] * S
    for l in range(S - 1, -1, -1):
        p = jnp.concatenate([pres[l, 0], pres[S - 1 - l, 1]])
        gh = parts[l, 2:4].reshape(2 * n, R).astype(F32)
        if l < S - 1:
            above = jnp.concatenate(grads[l + 1 :], axis=1)
            gh = gh + dot(above, mix[l, l + 1 :].reshape(-1, R), 1, 0)
        sig = jax.nn.sigmoid(p)
        hiddens[l] = (p * sig).astype(BF)
        grads[l] = (gh * sig * (1.0 + p * (1.0 - sig))).astype(BF)
    gp = jnp.stack(grads)
    hid = lax.dynamic_index_in_dim(jnp.stack(hiddens), k, 0, keepdims=False)
    gp_dn = lax.dynamic_index_in_dim(gp, k, 0, keepdims=False)[:n]
    gp_up = lax.dynamic_index_in_dim(gp, S - 1 - k, 0, keepdims=False)[n:]
    gp_dn = dot(order[0], gp_dn, 0, 0).astype(BF)
    gp_up = dot(order[1], gp_up, 0, 0).astype(BF)
    small = jnp.stack([gp_dn, gp_up, hid[:n], hid[n:]])
    small = lax.all_gather(small, "fsdp", axis=1, tiled=True)
    cross = lax.dot_general(gp, hid, (((1,), (0,)), ((), ())), preferred_element_type=F32)
    later = jnp.arange(S) > k
    cross = jnp.where(later[:, None, None], cross, 0.0).astype(BF)
    cross = lax.psum(cross, "fsdp")
    far_in = dot(xs[1], small[1], 0, 0).astype(BF)
    far_in = lax.ppermute(far_in, "section", [(i, S - 1 - i) for i in range(S)])
    grad_in = dot(xs[0], small[0], 0, 0) + far_in.astype(F32)
    grad_out = dot(small[2:].reshape(2 * N, R), gs.reshape(2 * N, -1), 0, 0)
    grad_out = grad_out + lax.dot_general(
        cross, w_all, (((0, 1), (0, 2)), ((), ())), preferred_element_type=F32
    )
    return (grad_in[None], grad_out[None])


def solution(mesh):
    in_specs = (
        P("section", "fsdp", None),
        P("section", None, "fsdp"),
        P("section", None, "fsdp", None),
        P("section", None, "fsdp", None),
        P(None, None, "fsdp", None),
        P(),
        P(),
        P(),
        P(),
    )
    out_specs = (P("section", "fsdp", None), P("section", None, "fsdp"))
    return jax.shard_map(
        on_device, mesh=mesh, in_specs=in_specs, out_specs=out_specs, check_vma=False
    )
```

time: 1060 us -> 309 us (0.29)
  waiting for transfers between devices: 406 us -> 145 us
  starting transfers between devices: 192 us -> 12.1 us
  matrix products: 199 us -> 21.7 us
  local copies, waits for them, and re-layouts: 151 us -> 60.8 us
  loops' own time: 47.9 us -> 0 us
  blocking collectives: 0 us -> 36.2 us
  other arithmetic: 47.8 us -> 15.5 us
    ppermute x44 -> x1, waiting for transfers between devices: 273 us -> 0.01 us  [on_device(): far_in = lax.ppermute(far_in, 'section', [(i, S - 1 - i) for i in range(S)])]
    ppermute x44 -> x1, starting transfers between devices: 192 us -> 1.78 us  [on_device(): far_in = lax.ppermute(far_in, 'section', [(i, S - 1 - i) for i in range(S)])]
    dot_general x120 -> x19, matrix products: 199 us -> 21.7 us  [the longest x15 11.4 us: dot(): lax.dot_general(a, b, (((ca,), (cb,)), ((), ())), preferred_element_type=...]
    cond x240 -> x0, local copies, waits for them, and re-layouts: 81.4 us -> none
    all_to_all x0 -> x2, waiting for transfers between devices: none -> 62.9 us  [the longest x1 32.9 us: on_device(): xs = lax.all_to_all(x, 'fsdp', split_axis=2, concat_axis=1, tiled=True)]
    another operation x39 -> x0, loops' own time: 47.9 us -> none  [the longest x38 47.1 us: slot_pass(): return lax.cond(valid, active, resting, state)]
    reduce_scatter x4 -> x2, waiting for transfers between devices: 82.6 us -> 37.3 us  [the longest x1 20.5 us: on_device(): parts = lax.psum_scatter(parts, 'fsdp', scatter_dimension=1, tiled=True)]
    all_gather x0 -> x2, blocking collectives: none -> 36.2 us  [the longest x1 29.7 us: on_device(): parts = lax.all_gather(parts, 'section', axis=0)]
  transfers between devices with their start and end apart: 52 -> 8, of which waited for: 35 -> 6; matrix products, arithmetic and copies ran while one was open for 17% -> 28% of each run, Pallas kernels for 0% -> 0%
where the time goes in v1:
time: 309 us; the launch traced here: 306 us
  waiting for transfers between devices  145 us (47%)
  local copies, waits for them, and re-layouts  60.8 us (20%)
  blocking collectives  36.2 us (12%)
  matrix products  21.7 us (7%)
  other arithmetic  15.5 us (5%)
  between operations  14.3 us (5%)
  starting transfers between devices  12.1 us (4%)
    all_to_all x1, waiting for transfers between devices, on_device(): xs = lax.all_to_all(x, 'fsdp', split_axis=2, concat_axis=1, tiled=True)  32.9 us
    all_to_all x1, waiting for transfers between devices, on_device(): lax.all_to_all(first.reshape(2, n, D), 'fsdp', split_axis=2, concat_axis=...  30 us
    all_gather x1, blocking collectives, on_device(): parts = lax.all_gather(parts, 'section', axis=0)  29.7 us
    all_gather x1, waiting for transfers between devices, on_device(): mix = lax.all_gather(mix, ('section', 'fsdp'), axis=0)  24.4 us
    reduce_scatter x1, waiting for transfers between devices, on_device(): parts = lax.psum_scatter(parts, 'fsdp', scatter_dimension=1, tiled=True)  20.5 us
    psum x1, waiting for transfers between devices, on_device(): cross = lax.psum(cross, 'fsdp')  19.6 us
    reduce_scatter x1, waiting for transfers between devices, on_device(): mix = lax.psum_scatter(mix, 'fsdp', scatter_dimension=1, tiled=True)  16.8 us
    all_to_all x2, local copies, waits for them, and re-layouts, on_device(): lax.all_to_all(first.reshape(2, n, D), 'fsdp', split_axis=2, concat_axis=...  15.3 us
  transfers between devices with their start and end apart: 8, of which 6 were waited for; matrix products, arithmetic and copies ran while one was open for 28% of the time, Pallas kernels for 0%

profile of v1, /device:TPU:8, one launch (start us, length us, event | category | flops | bytes accessed | tf_op | source)
XLA Modules:
  0.0 305.6 jit_solution(3300663985926334143)
XLA Ops:
  7.9 3.9 %pad_maximum_fusion = bf16[2,96,8192]{2,1,0:T(8,128)(2,1)} fusion(bf16[1,96,8192]{2,1,0:T(8,128)(2,1)} %bitcast.276, bf16[1,96,8192]{2,1,0:T(8,128)(2,1)} %bitcast.277), kind=kLoop, calls=%fused_computation.2 | loop fusion | flops 1572864 | bytes 6291456 | tf_op jit(solution)/shard_map/stack | solution.py:36
  11.8 9.8 %copy.161 = bf16[2,96,8192]{1,0,2:T(2,128)(2,1)} copy(bf16[2,96,8192]{2,1,0:T(8,128)(2,1)} %pad_maximum_fusion) | data formatting | bytes 6291456 | tf_op jit(solution)/shard_map/stack | solution.py:36
  21.6 5.1 %all-to-all-start = ((bf16[2,96,8192]{1,0,2:T(2,128)(2,1)}), bf16[2,96,8192]{1,0,2:T(2,128)(2,1)}, u32[]{:S(2)}, u32[]{:S(2)}) async-start(bf16[2,96,8192]{1,0,2:T(2,128)(2,1)} %copy.161), calls=%async_computation | async-start | bytes 8388608 | tf_op jit(solution)/shard_map/all_to_all | solution.py:37
  27.8 4.4 %fusion = bf16[2,96,8192]{2,1,0:T(8,128)(2,1)} fusion(bf16[2,12,8,8192]{3,2,1,0:T(8,128)(2,1)} %param.13, f32[8192]{0:T(1024)S(1)} %copy-done.5, f32[2,12,8]{2,1,0:T(8,128)S(1)} %copy.167), kind=kLoop, calls=%fused_computation.1 | loop fusion | flops 6291456 | bytes 6324992 | tf_op jit(solution)/shard_map/reshape | solution.py:54
  32.2 9.8 %copy.168 = bf16[2,96,8192]{1,0,2:T(2,128)(2,1)} copy(bf16[2,96,8192]{2,1,0:T(8,128)(2,1)} %fusion) | data formatting | bytes 6291456 | tf_op jit(solution)/shard_map/reshape | solution.py:54
  42.0 32.9 %all-to-all-done = bf16[2,96,8192]{1,0,2:T(2,128)(2,1)} async-done(((bf16[2,96,8192]{1,0,2:T(2,128)(2,1)}), bf16[2,96,8192]{1,0,2:T(2,128)(2,1)}, u32[]{:S(2)}, u32[]{:S(2)}) %all-to-all-start) | async-done | bytes 3145760 | tf_op jit(solution)/shard_map/all_to_all | solution.py:37
  74.9 4.9 %all-to-all-start.1 = ((bf16[2,96,8192]{1,0,2:T(2,128)(2,1)}), bf16[2,96,8192]{1,0,2:T(2,128)(2,1)}, u32[]{:S(2)}, u32[]{:S(2)}) async-start(bf16[2,96,8192]{1,0,2:T(2,128)(2,1)} %copy.168), calls=%async_computation.1 | async-start | bytes 8388608 | tf_op jit(solution)/shard_map/all_to_all | solution.py:53
  79.8 11.6 %copy.193 = bf16[2,96,4,2048]{3,2,1,0:T(4,128)(2,1)} copy(bf16[2,96,4,2048]{1,0,3,2:T(2,128)(2,1)} %bitcast.2) | data formatting | bytes 6291456 | tf_op jit(solution)/shard_map/all_to_all | solution.py:37
  91.4 4.6 %fusion.69 = (bf16[1,4,96,2048]{3,1,2,0:T(4,128)(2,1)}, bf16[1,4,96,2048]{3,1,2,0:T(4,128)(2,1)S(1)}) fusion(bf16[2,4,96,2048]{3,1,2,0:T(4,128)(2,1)} %bitcast.261), kind=kLoop, calls=%fused_computation.205 | loop fusion | bytes 6291456 | tf_op jit(solution)/shard_map/slice | solution.py:98
  96.0 2.0 copy.164
  98.0 30.0 %all-to-all-done.1 = bf16[2,96,8192]{1,0,2:T(2,128)(2,1)} async-done(((bf16[2,96,8192]{1,0,2:T(2,128)(2,1)}), bf16[2,96,8192]{1,0,2:T(2,128)(2,1)}, u32[]{:S(2)}, u32[]{:S(2)}) %all-to-all-start.1) | async-done | bytes 3145760 | tf_op jit(solution)/shard_map/all_to_all | solution.py:53
  128.0 11.5 %copy.194 = bf16[2,96,4,2048]{3,2,1,0:T(4,128)(2,1)} copy(bf16[2,96,4,2048]{1,0,3,2:T(2,128)(2,1)} %bitcast.12) | data formatting | bytes 6291456 | tf_op jit(solution)/shard_map/all_to_all | solution.py:53
  139.5 3.7 %copy.170 = bf16[2,4,96,2048]{3,2,1,0:T(8,128)(2,1)S(1)} copy(bf16[2,4,96,2048]{3,1,2,0:T(4,128)(2,1)} %bitcast.262) | data formatting | bytes 6291456 | tf_op jit(solution)/shard_map/all_to_all | solution.py:53
  145.2 4.2 %convolution_convert_fusion.1 = bf16[8,128,128]{2,1,0:T(8,128)(2,1)} fusion(bf16[8,2048,128]{2,1,0:T(8,128)(2,1)} %all-gather.5.cloned.1.call-done, bf16[1,128,2048]{2,1,0:T(8,128)(2,1)S(1)} %copy-done), kind=kOutput, calls=%fused_computation.11 | convolution fusion | flops 537001984 | bytes 4980736 | tf_op jit(solution)/shard_map/dot_general | solution.py:62
  150.1 2.1 fusion.4
  153.1 16.8 %reduce-scatter.5.cloned.1.call-done = bf16[8,32,128]{2,1,0:T(8,128)(2,1)} async-done(((bf16[8,128,128]{2,1,0:T(8,128)(2,1)}), bf16[8,32,128]{2,1,0:T(8,128)(2,1)}) %reduce-scatter.5.cloned.1.call-update) | async-done | bytes 65552 | tf_op jit(solution)/shard_map/reduce_scatter | solution.py:66
  173.5 20.5 %reduce-scatter.3.cloned.1.call-done = bf16[4,96,128]{2,1,0:T(8,128)(2,1)} async-done(((bf16[4,384,128]{2,1,0:T(8,128)(2,1)}), bf16[4,96,128]{2,1,0:T(8,128)(2,1)}) %reduce-scatter.3.cloned.1.call-update) | async-done | bytes 98320 | tf_op jit(solution)/shard_map/reduce_scatter | solution.py:65
  194.0 29.7 %all-gather = bf16[32,96,128]{2,1,0:T(8,128)(2,1)S(1)} all-gather(bf16[4,96,128]{2,1,0:T(8,128)(2,1)} %reduce-scatter.3.cloned.1.call-done), channel_id=2, replica_groups=mesh['section'=8,'fsdp'=4] {'section'}, dimensions={0}, use_global_device_ids=true | all-gather | bytes 884736 | tf_op jit(solution)/shard_map/all_gather | solution.py:67
  228.9 24.4 %all-gather.7.cloned.1.call-done = bf16[256,32,128]{2,1,0:T(8,128)(2,1)} async-done(((bf16[8,32,128]{2,1,0:T(8,128)(2,1)}), bf16[256,32,128]{2,1,0:T(8,128)(2,1)}) %all-gather.7.cloned.1.call-update) | async-done | bytes 2097168 | tf_op jit(solution)/shard_map/all_gather | solution.py:68
  253.3 2.2 copy.175
  261.2 6.5 %all_gather.23 = bf16[4,384,128]{2,1,0:T(8,128)(2,1)S(1)} all-gather(bf16[4,96,128]{2,1,0:T(8,128)(2,1)S(1)} %pad_maximum_fusion.18), channel_id=1, replica_groups=mesh['section'=8,'fsdp'=4] {'fsdp'}, dimensions={1}, use_global_device_ids=true | all-gather | bytes 491520 | tf_op jit(solution)/shard_map/all_gather | solution.py:91
  267.7 2.8 convolution_convert_fusion
  272.4 19.6 %all-reduce.2.cloned.1.call-done = bf16[8,128,128]{2,1,0:T(8,128)(2,1)} async-done(((bf16[8,128,128]{2,1,0:T(8,128)(2,1)}), bf16[8,128,128]{2,1,0:T(8,128)(2,1)}) %all-reduce.2.cloned.1.call-update) | async-done | bytes 262160 | tf_op jit(solution)/shard_map/psum | solution.py:95
  292.0 3.9 %convolution_bitcast_fusion = f32[128,2048]{1,0:T(8,128)S(1)} fusion(bf16[8,128,128]{2,1,0:T(8,128)(2,1)} %all-reduce.2.cloned.1.call-done, bf16[8,2048,128]{2,1,0:T(8,128)(2,1)} %all-gather.5.cloned.1.call-done), kind=kOutput, calls=%fused_computation.3 | convolution fusion | flops 536870912 | bytes 5505024 | tf_op jit(solution)/shard_map/dot_general | solution.py:100
  (109 shorter events, 24.4 us)
Async XLA Ops:
  7.2 137.0 %copy-start = (bf16[1,128,2048]{2,1,0:T(8,128)(2,1)S(1)}, bf16[1,128,2048]{2,1,0:T(8,128)(2,1)}, u32[]{:S(2)}) copy-start(bf16[1,128,2048]{2,1,0:T(8,128)(2,1)} %param.10) | copy-start | bytes 1572868
  7.2 138.0 %all-gather.5.cloned.1.call-start = ((), (), s32[]{:S(2)}) async-start(), calls=%async_computation.4 | async-start | bytes 4718592 | tf_op jit(solution)/shard_map/all_gather | solution.py:38
  21.5 5.1 %copy-start.8 = (s32[2,12]{1,0:T(2,128)S(1)}, s32[2,12]{1,0:T(2,128)}, u32[]{:S(2)}) copy-start(s32[2,12]{1,0:T(2,128)} %param.14) | copy-start | bytes 292
  21.5 5.2 %copy-start.6 = (s32[2,12,4]{1,2,0:T(4,128)S(1)}, s32[2,12,4]{1,2,0:T(4,128)}, u32[]{:S(2)}) copy-start(s32[2,12,4]{1,2,0:T(4,128)} %param.15) | copy-start | bytes 1156
  21.6 5.8 %copy-start.7 = (f32[2,12,4]{1,2,0:T(4,128)S(1)}, f32[2,12,4]{1,2,0:T(4,128)}, u32[]{:S(2)}) copy-start(f32[2,12,4]{1,2,0:T(4,128)} %param.16) | copy-start | bytes 1156
  21.6 6.2 %copy-start.5 = (f32[8192]{0:T(1024)S(1)}, f32[8192]{0:T(1024)}, u32[]{:S(2)}) copy-start(f32[8192]{0:T(1024)} %param.17) | copy-start | bytes 98308
  21.6 53.3 %all-to-all-start = ((bf16[2,96,8192]{1,0,2:T(2,128)(2,1)}), bf16[2,96,8192]{1,0,2:T(2,128)(2,1)}, u32[]{:S(2)}, u32[]{:S(2)}) async-start(bf16[2,96,8192]{1,0,2:T(2,128)(2,1)} %copy.161), calls=%async_computation | async-start | bytes 8388608 | tf_op jit(solution)/shard_map/all_to_all | solution.py:37
  74.9 53.2 %all-to-all-start.1 = ((bf16[2,96,8192]{1,0,2:T(2,128)(2,1)}), bf16[2,96,8192]{1,0,2:T(2,128)(2,1)}, u32[]{:S(2)}, u32[]{:S(2)}) async-start(bf16[2,96,8192]{1,0,2:T(2,128)(2,1)} %copy.168), calls=%async_computation.1 | async-start | bytes 8388608 | tf_op jit(solution)/shard_map/all_to_all | solution.py:53
  79.8 90.1 %reduce-scatter.5.cloned.1.call-start = ((), (), s32[]{:S(2)}) async-start(), calls=%async_computation.6 | async-start | bytes 327680 | tf_op jit(solution)/shard_map/reduce_scatter | solution.py:66
  139.5 3.7 %copy-start.3 = (bf16[1,4,96,2048]{3,1,2,0:T(4,128)(2,1)S(1)}, bf16[1,4,96,2048]{3,1,2,0:T(4,128)(2,1)}, u32[]{:S(2)}) copy-start(bf16[1,4,96,2048]{3,1,2,0:T(4,128)(2,1)} %get-tuple-element.2) | copy-start | bytes 4718596
  143.3 1.9 copy-start.1
  145.2 4.4 %copy-start.4 = (bf16[1,2048,128]{2,1,0:T(8,128)(2,1)S(1)}, bf16[1,2048,128]{2,1,0:T(8,128)(2,1)}, u32[]{:S(2)}) copy-start(bf16[1,2048,128]{2,1,0:T(8,128)(2,1)} %param.9) | copy-start | bytes 1572868
  149.5 44.5 %reduce-scatter.3.cloned.1.call-start = ((), (), s32[]{:S(2)}) async-start(), calls=%async_computation.5 | async-start | bytes 491520 | tf_op jit(solution)/shard_map/reduce_scatter | solution.py:65
  153.1 100.2 %all-gather.7.cloned.1.call-start = ((), (), s32[]{:S(2)}) async-start(), calls=%async_computation.8 | async-start | bytes 2162688 | tf_op jit(solution)/shard_map/all_gather | solution.py:68
  169.9 122.0 %all-reduce.2.cloned.1.call-start = ((), (), s32[]{:S(2)}) async-start(), calls=%async_computation.7 | async-start | bytes 524288 | tf_op jit(solution)/shard_map/psum | solution.py:95
  270.6 26.9 %collective-permute-start = (bf16[2048,128]{1,0:T(8,128)(2,1)}, bf16[2048,128]{1,0:T(8,128)(2,1)S(1)}, u32[]{:S(2)}, u32[]{:S(2)}) collective-permute-start(bf16[2048,128]{1,0:T(8,128)(2,1)} %convolution_convert_fusion), channel_id=1, source_target_pairs={{0,28},{4,24},{8,20},{12,16},{16,12},{20,8},{24,4},{28,0},{1,29},{... | collective-permute-start | bytes 1572872 | tf_op jit(solution)/shard_map/ppermute | solution.py:97
  291.9 3.9 %copy-start.2 = (bf16[2,4,96,2048]{3,2,1,0:T(8,128)(2,1)S(1)}, bf16[2,4,96,2048]{3,2,1,0:T(8,128)(2,1)}, u32[]{:S(2)}) copy-start(bf16[2,4,96,2048]{3,2,1,0:T(8,128)(2,1)} %copy-done.1) | copy-start | bytes 9437188
Sparse Core Ops, SparseCore 0:
  10.1 73.8 all-gather.4
  149.6 20.2 reduce-scatter.4
  173.1 20.8 reduce-scatter.2
  197.1 56.1 all-gather.6
  260.2 31.6 all-reduce.1

commit v2 on v1

v2 whole, which is shorter than its diff:
```python
import functools

import jax
import jax.numpy as jnp
from jax import lax
from jax.experimental import pallas as pl
from jax.experimental.pallas import tpu as pltpu
from jax.sharding import PartitionSpec as P

BF = jnp.bfloat16
F32 = jnp.float32
MESH = pl.DeviceIdType.MESH


def dot(a, b, ca, cb):
    return lax.dot_general(a, b, (((ca,), (cb,)), ((), ())), preferred_element_type=F32)


def kernel(
    S, F,
    xd_ref, xu_ref, win_ref, wout_ref, top_ref, roww_ref, head_ref, order_ref,
    gin_ref, gout_ref,
    xs, wo, wall, gf, gs, pp, pr, mp, mr, mt, farp, farr, gp, hid, smd, smu, cs, cr,
    gfar, gfr, acc, ds,
    s_loc, s_xs, s_xr, s_wos, s_wor, s_ws, s_wr, s_gs, s_gr, s_ps, s_pr, s_ms, s_mr,
    s_f, s_gps, s_gpr, s_hs, s_hr, s_ds, s_dr, s_us, s_ur, s_cs, s_cr, s_e,
):
    k = lax.axis_index("section")
    f = lax.axis_index("fsdp")
    mir = S - 1 - k
    n, R, Ds = xs.shape[2], wall.shape[2], wall.shape[1]
    Z = S // 2
    z, y = k // 2, k % 2

    def rc(src, dst, ss, rs, dev):
        return pltpu.make_async_remote_copy(
            src_ref=src, dst_ref=dst, send_sem=ss, recv_sem=rs, device_id=dev, device_id_type=MESH
        )

    peers = [lax.rem(f + j, F) for j in range(1, F)]

    barrier = pltpu.get_barrier_semaphore()
    for p in peers:
        pl.semaphore_signal(barrier, inc=1, device_id=(k, p), device_id_type=MESH)
    for j in range(1, S):
        pl.semaphore_signal(
            barrier, inc=1, device_id=(lax.rem(k + j, S), f), device_id_type=MESH
        )
    pl.semaphore_wait(barrier, S - 1 + F - 1)

    def cols(p):
        return pl.ds(pl.multiple_of(p * Ds, Ds), Ds)

    def x_copies(p, j):
        return [
            rc(xd_ref.at[:, cols(p)], xs.at[0, f], s_xs.at[0, j], s_xr.at[0, f], (k, p)),
            rc(xu_ref.at[:, cols(p)], xs.at[1, f], s_xs.at[1, j], s_xr.at[1, f], (k, p)),
        ]

    def wo_copy(p, j):
        return rc(wout_ref, wo.at[f], s_wos.at[j], s_wor.at[f], (k, p))

    def w_copy(src, s, way):
        dev = [(k + 2, f), (k - 2, f), (k + 1 - 2 * y, f)][way]
        return rc(src, wall.at[s], s_ws.at[s, way], s_wr.at[s], dev)

    local = [
        pltpu.make_async_copy(win_ref, wall.at[k], s_loc.at[0]),
        pltpu.make_async_copy(wout_ref, wo.at[f], s_loc.at[1]),
        pltpu.make_async_copy(xd_ref.at[:, cols(f)], xs.at[0, f], s_loc.at[2]),
        pltpu.make_async_copy(xu_ref.at[:, cols(f)], xs.at[1, f], s_loc.at[3]),
    ]

    @pl.when(z < Z - 1)
    def _():
        w_copy(win_ref, k, 0).start()

    @pl.when(z > 0)
    def _():
        w_copy(win_ref, k, 1).start()

    w_copy(win_ref, k, 2).start()
    for j, p in enumerate(peers):
        for c in x_copies(p, j):
            c.start()
    for c in local:
        c.start()
    for j, p in enumerate(peers):
        wo_copy(p, j).start()

    @pl.loop(0, F)
    def _(c):
        block = top_ref[:, cols(c)].astype(F32) + roww_ref[...] * head_ref[:, cols(c)]
        gf[c] = block.astype(BF)

    gs[f] = gf[f]

    for t in range(1, Z):
        lo, hi = k - 2 * t, k + 2 * t

        @pl.when(z - t >= 0)
        def _():
            w_copy(wall.at[lo], lo, 0).wait_recv()

            @pl.when(z < Z - 1)
            def _():
                w_copy(wall.at[lo], lo, 0).start()

            w_copy(wall.at[lo], lo, 2).start()

        @pl.when(z + t < Z)
        def _():
            w_copy(wall.at[hi], hi, 1).wait_recv()

            @pl.when(z > 0)
            def _():
                w_copy(wall.at[hi], hi, 1).start()

            w_copy(wall.at[hi], hi, 2).start()

    for c in local:
        c.wait()

    @pl.loop(0, Z)
    def _(t):
        s = 2 * t + 1 - y
        w_copy(wall.at[s], s, 2).wait_recv()

    def pp_copy(p, j):
        return rc(pp.at[p], pr.at[f], s_ps.at[j], s_pr.at[f], (k, p))

    def pre_part(p):
        a = dot(xs[0, p], wall[k], 1, 0)
        b = dot(xs[1, p], wall[mir], 1, 0)
        pp[p, 0] = a.astype(BF)
        pp[p, 1] = b.astype(BF)

    def m_copy(p, j):
        return rc(mp, mr.at[f], s_ms.at[j], s_mr.at[f], (k, p))

    @pl.loop(0, S)
    def _(s):
        mp[s] = dot(wout_ref[...], wall[s], 1, 0).astype(BF)

    for j, p in enumerate(peers):
        m_copy(p, j).start()
    pre_part(f)

    @pl.loop(1, F)
    def _(j):
        p = lax.rem(f + j, F)
        rc(xs.at[0, p], xs.at[0, p], s_xs.at[0, 0], s_xr.at[0, p], (k, p)).wait_recv()
        rc(xs.at[1, p], xs.at[1, p], s_xs.at[1, 0], s_xr.at[1, p], (k, p)).wait_recv()
        pre_part(p)
        pp_copy(p, j - 1).start()

    acc[...] = dot(gf[f], wo[f], 1, 1)

    @pl.loop(1, F)
    def _(j):
        p = lax.rem(f + j, F)
        rc(wo.at[p], wo.at[p], s_wos.at[0], s_wor.at[p], (k, p)).wait_recv()
        acc[...] += dot(gf[p], wo[p], 1, 1)

    pd = pp[f, 0].astype(F32)
    pu = pp[f, 1].astype(F32)
    for p in peers:
        rc(pr.at[p], pr.at[p], s_ps.at[0], s_pr.at[p], (k, p)).wait_recv()
        pd = pd + pr[p, 0].astype(F32)
        pu = pu + pr[p, 1].astype(F32)
    farp[...] = dot(order_ref[1], pu.astype(BF), 1, 0).astype(BF)
    far_copy = rc(farp, farr, s_f.at[0], s_f.at[1], (mir, f))
    far_copy.start()

    def g_copy(p, j):
        return rc(gf.at[p], gs.at[f], s_gs.at[j], s_gr.at[f], (k, p))

    for j, p in enumerate(peers):
        g_copy(p, j).start()

    def gate(rows, pre):
        sig = jax.nn.sigmoid(pre)
        hid[f, rows] = (pre * sig).astype(BF)
        ds[rows] = sig * (1.0 + pre * (1.0 - sig))

    gate(pl.ds(0, n), dot(order_ref[0], pd.astype(BF), 1, 0))

    for p in peers:
        rc(mr.at[p], mr.at[p], s_ms.at[0], s_mr.at[p], (k, p)).wait_recv()

    @pl.loop(0, S)
    def _(s):
        total = mp[s].astype(F32)
        for p in peers:
            total = total + mr[p, s].astype(F32)
        mt[s] = total.astype(BF)

    far_copy.wait_recv()
    gate(pl.ds(n, n), farr[...].astype(F32))

    def h_copy(p, j):
        return rc(hid.at[f], hid.at[f], s_hs.at[j], s_hr.at[f], (k, p))

    for j, p in enumerate(peers):
        h_copy(p, j).start()

    def gp_copy(to):
        return rc(gp.at[k], gp.at[k], s_gps.at[to], s_gpr.at[k], (to, f))

    def gp_arrived(s):
        rc(gp.at[s], gp.at[s], s_gps.at[0], s_gpr.at[s], (s, f)).wait_recv()

    def finish():
        gp[k] = (acc[...] * ds[...]).astype(BF)

        @pl.loop(0, k)
        def _(i):
            gp_copy(k - 1 - i).start()

        @pl.when(mir > k)
        def _():
            gp_copy(mir).start()

    def c_copy(s, p, j):
        return rc(cs.at[s], cr.at[f, s], s_cs.at[s, j], s_cr.at[f, s], (k, p))

    @pl.when(k == S - 1)
    def _():
        finish()

    @pl.loop(0, S - 1 - k)
    def _(i):
        s = S - 1 - i
        gp_arrived(s)
        acc[...] += dot(gp[s], mt[s], 1, 1)

        @pl.when(s == k + 1)
        def _():
            finish()

        cs[s] = dot(hid[f], gp[s], 0, 0).astype(BF)
        for j, p in enumerate(peers):
            c_copy(s, p, j).start()

    def d_copy(p, j):
        return rc(smd.at[f], smd.at[f], s_ds.at[j], s_dr.at[f], (k, p))

    def u_copy(p, j):
        return rc(smu.at[f], smu.at[f], s_us.at[j], s_ur.at[f], (k, p))

    smd[f] = dot(order_ref[0], gp[k, pl.ds(0, n)], 0, 0).astype(BF)
    for j, p in enumerate(peers):
        d_copy(p, j).start()

    @pl.when(mir < k)
    def _():
        gp_arrived(mir)

    smu[f] = dot(order_ref[1], gp[mir, pl.ds(n, n)], 0, 0).astype(BF)
    for j, p in enumerate(peers):
        u_copy(p, j).start()
    for p in peers:
        rc(smu.at[p], smu.at[p], s_us.at[0], s_ur.at[p], (k, p)).wait_recv()
        rc(smd.at[p], smd.at[p], s_ds.at[0], s_dr.at[p], (k, p)).wait_recv()

    gin_ref[...] = dot(xs[1, 0], smu[0], 0, 0)

    @pl.loop(1, F)
    def _(c):
        gin_ref[...] += dot(xs[1, c], smu[c], 0, 0)

    gfar[...] = gin_ref[...].astype(BF)
    e_copy = rc(gfar, gfr, s_e.at[0], s_e.at[1], (mir, f))
    e_copy.start()

    gin_ref[...] = dot(xs[0, 0], smd[0], 0, 0)

    @pl.loop(1, F)
    def _(c):
        gin_ref[...] += dot(xs[0, c], smd[c], 0, 0)

    gout_ref[...] = dot(hid[f], gs[f], 0, 0)

    @pl.loop(1, F)
    def _(j):
        p = lax.rem(f + j, F)
        rc(hid.at[p], hid.at[p], s_hs.at[0], s_hr.at[p], (k, p)).wait_recv()
        rc(gs.at[p], gs.at[p], s_gs.at[0], s_gr.at[p], (k, p)).wait_recv()
        gout_ref[...] += dot(hid[p], gs[p], 0, 0)

    @pl.loop(0, S - 1 - k)
    def _(i):
        s = S - 1 - i
        total = cs[s].astype(F32)
        for p in peers:
            rc(cr.at[p, s], cr.at[p, s], s_cs.at[s, 0], s_cr.at[p, s], (k, p)).wait_recv()
            total = total + cr[p, s].astype(F32)
        gout_ref[...] += dot(total.astype(BF), wall[s], 1, 1)

    e_copy.wait_recv()
    gin_ref[...] += gfr[...].astype(F32)

    for j, p in enumerate(peers):
        for c in x_copies(p, j):
            c.wait_send()
        for c in (wo_copy, m_copy, pp_copy, g_copy, h_copy, d_copy, u_copy):
            c(p, j).wait_send()

    @pl.loop(0, S - 1 - k)
    def _(i):
        s = S - 1 - i
        for j, p in enumerate(peers):
            c_copy(s, p, j).wait_send()

    far_copy.wait_send()
    e_copy.wait_send()

    @pl.loop(0, k)
    def _(i):
        gp_copy(i).wait_send()

    @pl.when(mir > k)
    def _():
        gp_copy(mir).wait_send()

    for t in range(0, Z):
        lo, hi = k - 2 * t, k + 2 * t

        @pl.when(z - t >= 0)
        def _():
            @pl.when(z < Z - 1)
            def _():
                w_copy(wall.at[lo], lo, 0).wait_send()

            w_copy(wall.at[lo], lo, 2).wait_send()

        if t > 0:

            @pl.when(z + t < Z)
            def _():
                @pl.when(z > 0)
                def _():
                    w_copy(wall.at[hi], hi, 1).wait_send()

                w_copy(wall.at[hi], hi, 2).wait_send()

        else:

            @pl.when(z > 0)
            def _():
                w_copy(wall.at[hi], hi, 1).wait_send()


def on_device(
    branch_in,
    branch_out,
    down_inputs,
    up_inputs,
    top_grads,
    plan,
    reward_pos,
    reward_cot,
    reward_head,
):
    S = lax.axis_size("section")
    F = lax.axis_size("fsdp")
    f = lax.axis_index("fsdp")
    _, micro, r, D = down_inputs.shape
    n = micro * r
    seqs = reward_pos.shape[2]
    seq_len = r * F // seqs
    w_in, w_out = branch_in[0], branch_out[0]
    Ds, R = w_in.shape

    row_global = f * r + jnp.arange(r, dtype=jnp.int32)
    pick = plan[:, :, None] == jnp.arange(micro, dtype=jnp.int32)
    pos = jnp.sum(jnp.where(pick[..., None], reward_pos[:, None], 0), axis=2)
    cot = jnp.sum(jnp.where(pick[..., None], reward_cot[:, None], 0.0), axis=2)
    target = jnp.arange(seqs, dtype=jnp.int32) * seq_len + pos
    weight = jnp.sum(jnp.where(target[..., None] == row_global, cot[..., None], 0.0), axis=2)
    row = jnp.arange(n, dtype=jnp.int32)
    match = jnp.repeat(plan, r, axis=1) * r + row % r
    order = (match[:, :, None] == row).astype(BF)

    vm = pltpu.VMEM
    dma = pltpu.SemaphoreType.DMA
    anyspec = pl.BlockSpec(memory_space=pl.ANY)
    vspec = pl.BlockSpec(memory_space=pltpu.VMEM)
    gin, gout = pl.pallas_call(
        functools.partial(kernel, S, F),
        out_shape=(
            jax.ShapeDtypeStruct((Ds, R), F32),
            jax.ShapeDtypeStruct((R, Ds), F32),
        ),
        in_specs=[anyspec, anyspec, vspec, vspec, vspec, vspec, vspec, vspec],
        out_specs=(vspec, vspec),
        scratch_shapes=[
            vm((2, F, n, Ds), BF),
            vm((F, R, Ds), BF),
            vm((S, Ds, R), BF),
            vm((F, 2 * n, Ds), BF),
            vm((F, 2 * n, Ds), BF),
            vm((F, 2, n, R), BF),
            vm((F, 2, n, R), BF),
            vm((S, R, R), BF),
            vm((F, S, R, R), BF),
            vm((S, R, R), BF),
            vm((n, R), BF),
            vm((n, R), BF),
            vm((S, 2 * n, R), BF),
            vm((F, 2 * n, R), BF),
            vm((F, n, R), BF),
            vm((F, n, R), BF),
            vm((S, R, R), BF),
            vm((F, S, R, R), BF),
            vm((Ds, R), BF),
            vm((Ds, R), BF),
            vm((2 * n, R), F32),
            vm((2 * n, R), F32),
            dma((4,)),
            dma((2, F)), dma((2, F)),
            dma((F,)), dma((F,)),
            dma((S, 3)), dma((S,)),
            dma((F,)), dma((F,)),
            dma((F,)), dma((F,)),
            dma((F,)), dma((F,)),
            dma((2,)),
            dma((S,)), dma((S,)),
            dma((F,)), dma((F,)),
            dma((F,)), dma((F,)),
            dma((F,)), dma((F,)),
            dma((S, F)), dma((F, S)),
            dma((2,)),
        ],
        compiler_params=pltpu.CompilerParams(
            collective_id=0, has_side_effects=True, vmem_limit_bytes=54 * 2**20
        ),
        cost_estimate=pl.CostEstimate(
            flops=16 * F * n * Ds * R, bytes_accessed=16 * n * D, transcendentals=2 * n * R
        ),
    )(
        down_inputs.reshape(n, D),
        up_inputs.reshape(n, D),
        w_in,
        w_out,
        top_grads.reshape(2 * n, D),
        weight.reshape(2 * n, 1),
        reward_head.reshape(1, D),
        order,
    )
    return (gin[None], gout[None])


def solution(mesh):
    in_specs = (
        P("section", "fsdp", None),
        P("section", None, "fsdp"),
        P("section", None, "fsdp", None),
        P("section", None, "fsdp", None),
        P(None, None, "fsdp", None),
        P(),
        P(),
        P(),
        P(),
    )
    out_specs = (P("section", "fsdp", None), P("section", None, "fsdp"))
    return jax.shard_map(
        on_device, mesh=mesh, in_specs=in_specs, out_specs=out_specs, check_vma=False
    )
```

time: 309 us -> 162 us (0.52)
  Pallas kernels: 0 us -> 151 us
  waiting for transfers between devices: 145 us -> 0 us
  local copies, waits for them, and re-layouts: 60.8 us -> 4.49 us
  blocking collectives: 36.2 us -> 0 us
  matrix products: 21.7 us -> 0 us
  between operations: 14.3 us -> 0.7 us
  starting transfers between devices: 12.1 us -> 0 us
  other arithmetic: 15.5 us -> 4.28 us
    pallas_call x0 -> x1, Pallas kernels: none -> 151 us  [on_device(): pl.pallas_call(functools.partial(kernel, S, F), out_shape=(jax.ShapeDtype...]
    all_to_all x2 -> x0, waiting for transfers between devices: 62.9 us -> none  [the longest x1 32.9 us: on_device(): xs = lax.all_to_all(x, 'fsdp', split_axis=2, concat_axis=1, tiled=True)]
    reduce_scatter x2 -> x0, waiting for transfers between devices: 37.3 us -> none  [the longest x1 20.5 us: on_device(): parts = lax.psum_scatter(parts, 'fsdp', scatter_dimension=1, tiled=True)]
    all_gather x2 -> x0, blocking collectives: 36.2 us -> none  [the longest x1 29.7 us: on_device(): parts = lax.all_gather(parts, 'section', axis=0)]
    all_to_all x3 -> x0, local copies, waits for them, and re-layouts: 26.8 us -> none  [the longest x2 15.3 us: on_device(): lax.all_to_all(first.reshape(2, n, D), 'fsdp', split_axis=2, concat_axis=...]
    all_gather x2 -> x0, waiting for transfers between devices: 24.4 us -> none  [the longest x1 24.4 us: on_device(): mix = lax.all_gather(mix, ('section', 'fsdp'), axis=0)]
    dot_general x19 -> x0, matrix products: 21.7 us -> none  [the longest x15 11.4 us: dot(): lax.dot_general(a, b, (((ca,), (cb,)), ((), ())), preferred_element_type=...]
    psum x1 -> x0, waiting for transfers between devices: 19.6 us -> none  [on_device(): cross = lax.psum(cross, 'fsdp')]
  transfers between devices with their start and end apart: 8 -> 0, of which waited for: 6 -> 0; matrix products, arithmetic and copies ran while one was open for 28% -> 0% of each run, Pallas kernels for 0% -> 0%
where the time goes in v2:
time: 162 us; the launch traced here: 161 us
  Pallas kernels  151 us (93%)
  local copies, waits for them, and re-layouts  4.49 us (3%)
  other arithmetic  4.28 us (3%)
    pallas_call x1, Pallas kernels, on_device(): pl.pallas_call(functools.partial(kernel, S, F), out_shape=(jax.ShapeDtype...  151 us
    unnamed x4, local copies, waits for them, and re-layouts  3.32 us

profile of v2, /device:TPU:8, one launch (start us, length us, event | category | flops | bytes accessed | tf_op | source)
XLA Modules:
  0.0 160.7 jit_solution(4759084236683436819)
XLA Ops:
  0.7 0.7 broadcast_multiply_fusion
  1.3 0.8 iota_compare_fusion.1
  2.1 0.1 broadcast_in_dim.79
  2.2 0.1 mul.28
  2.3 0.8 select_reduce_fusion
  3.1 0.1 copy.21
  3.2 1.2 select_reduce_fusion.1
  4.3 0.1 copy.20
  4.4 0.1 broadcast_add_fusion
  4.5 0.1 select_reduce_fusion.2
  4.6 0.1 copy.22
  4.7 0.7 fusion.order_ref
  5.4 0.7 reshape.72.roww_ref
  6.1 151.2 %shard_map.104 = (f32[2048,128]{1,0:T(8,128)}, f32[128,2048]{1,0:T(8,128)}) custom-call(bf16[96,8192]{1,0:T(8,128)(2,1)} %bitcast.9, bf16[96,8192]{1,0:T(8,128)(2,1)} %bitcast.10, bf16[2048,128]{1,0:T(8,128)(2,1)} %bitcast.13, bf16[128,2048]{1,0:T(8,128)(2,1)} %bitcast.14, bf16[192,8192]{1,0:T(8,128)(2,1)} %bitcast.8, f32[192,1]{1,0:T(8,128)} %reshape.72.roww_ref, ...), custom_call_target="tpu_custom_call" | custom-call | flops 1610612736 | bytes 12582912 | tf_op jit(solution)/shard_map/pallas_call | solution.py:389
  157.3 0.0 copy-start
  157.3 2.4 %copy.26 = f32[1,2048,128]{2,1,0:T(8,128)} copy(f32[1,2048,128]{2,1,0:T(8,128)} %bitcast.12) | data formatting | bytes 2097152
  159.7 0.0 copy-done
  159.7 1.0 copy.27
  (4 shorter events, 0.0 us)
Async XLA Ops:
  157.3 2.4 %copy-start = (f32[128,2048]{1,0:T(8,128)S(1)}, f32[128,2048]{1,0:T(8,128)}, u32[]{:S(2)}) copy-start(f32[128,2048]{1,0:T(8,128)} %get-tuple-element.5) | copy-start | bytes 3145732

commit v3 on v2

--- a/solution.py
+++ b/solution.py
@@ -22,7 +22,7 @@
     gin_ref, gout_ref,
     xs, wo, wall, gf, gs, pp, pr, mp, mr, mt, farp, farr, gp, hid, smd, smu, cs, cr,
     gfar, gfr, acc, ds,
-    s_loc, s_xs, s_xr, s_wos, s_wor, s_ws, s_wr, s_gs, s_gr, s_ps, s_pr, s_ms, s_mr,
+    s_loc, s_xs, s_xr, s_wos, s_wof, s_wor, s_ws, s_wr, s_gs, s_gf, s_gr, s_ps, s_pr, s_ms, s_mr,
     s_f, s_gps, s_gpr, s_hs, s_hr, s_ds, s_dr, s_us, s_ur, s_cs, s_cr, s_e,
 ):
     k = lax.axis_index("section")
@@ -37,7 +37,13 @@
             src_ref=src, dst_ref=dst, send_sem=ss, recv_sem=rs, device_id=dev, device_id_type=MESH
         )
 
-    peers = [lax.rem(f + j, F) for j in range(1, F)]
+    core, chips = f % 2, F // 2
+    sib, across = f + 1 - 2 * core, k + 1 - 2 * y
+    peers = [sib]
+    for j in range(1, chips):
+        chip = lax.rem(f // 2 + j, chips)
+        peers += [2 * chip + core, 2 * chip + 1 - core]
+    same = list(range(1, F - 1, 2))
 
     barrier = pltpu.get_barrier_semaphore()
     for p in peers:
@@ -85,8 +91,8 @@
             c.start()
     for c in local:
         c.start()
-    for j, p in enumerate(peers):
-        wo_copy(p, j).start()
+    for j in [0] + same:
+        wo_copy(peers[j], j).start()
 
     @pl.loop(0, F)
     def _(c):
@@ -127,7 +133,7 @@
         w_copy(wall.at[s], s, 2).wait_recv()
 
     def pp_copy(p, j):
-        return rc(pp.at[p], pr.at[f], s_ps.at[j], s_pr.at[f], (k, p))
+        return rc(pp.at[p], pr.at[f], s_ps.at[p], s_pr.at[f], (k, p))
 
     def pre_part(p):
         a = dot(xs[0, p], wall[k], 1, 0)
@@ -135,15 +141,6 @@
         pp[p, 0] = a.astype(BF)
         pp[p, 1] = b.astype(BF)
 
-    def m_copy(p, j):
-        return rc(mp, mr.at[f], s_ms.at[j], s_mr.at[f], (k, p))
-
-    @pl.loop(0, S)
-    def _(s):
-        mp[s] = dot(wout_ref[...], wall[s], 1, 0).astype(BF)
-
-    for j, p in enumerate(peers):
-        m_copy(p, j).start()
     pre_part(f)
 
     @pl.loop(1, F)
@@ -154,12 +151,45 @@
         pre_part(p)
         pp_copy(p, j - 1).start()
 
+    def wo_pass(j):
+        p = peers[j]
+        return rc(wo.at[p], wo.at[p], s_wof.at[j], s_wor.at[p], (k, sib))
+
+    for j in same:
+        p = peers[j]
+        rc(wo.at[p], wo.at[p], s_wos.at[0], s_wor.at[p], (k, p)).wait_recv()
+        wo_pass(j).start()
+
+    def rows(d):
+        return pl.ds(pl.multiple_of(d * n, 16), n)
+
+    def g_copy(p, j):
+        return rc(gf.at[p, rows(y)], gs.at[f, rows(y)], s_gs.at[j], s_gr.at[y, f], (k, p))
+
+    g_sib = rc(
+        gf.at[sib, rows(1 - y)], gs.at[f, rows(1 - y)], s_gs.at[F - 1], s_gr.at[1 - y, f], (k, sib)
+    )
+
+    def g_pass(j):
+        p = peers[j]
+        return rc(
+            gs.at[p, rows(y)], gs.at[p, rows(y)], s_gf.at[j], s_gr.at[y, p], (across, f)
+        )
+
+    for j, p in enumerate(peers):
+        g_copy(p, j).start()
+    g_sib.start()
+
     acc[...] = dot(gf[f], wo[f], 1, 1)
 
     @pl.loop(1, F)
     def _(j):
         p = lax.rem(f + j, F)
-        rc(wo.at[p], wo.at[p], s_wos.at[0], s_wor.at[p], (k, p)).wait_recv()
+
+        @pl.when(jnp.logical_or(p == sib, p % 2 != core))
+        def _():
+            rc(wo.at[p], wo.at[p], s_wos.at[0], s_wor.at[p], (k, p)).wait_recv()
+
         acc[...] += dot(gf[p], wo[p], 1, 1)
 
     pd = pp[f, 0].astype(F32)
@@ -172,28 +202,22 @@
     far_copy = rc(farp, farr, s_f.at[0], s_f.at[1], (mir, f))
     far_copy.start()
 
-    def g_copy(p, j):
-        return rc(gf.at[p], gs.at[f], s_gs.at[j], s_gr.at[f], (k, p))
-
-    for j, p in enumerate(peers):
-        g_copy(p, j).start()
-
-    def gate(rows, pre):
+    def gate(at, pre):
         sig = jax.nn.sigmoid(pre)
-        hid[f, rows] = (pre * sig).astype(BF)
-        ds[rows] = sig * (1.0 + pre * (1.0 - sig))
+        hid[f, at] = (pre * sig).astype(BF)
+        ds[at] = sig * (1.0 + pre * (1.0 - sig))
 
     gate(pl.ds(0, n), dot(order_ref[0], pd.astype(BF), 1, 0))
 
-    for p in peers:
-        rc(mr.at[p], mr.at[p], s_ms.at[0], s_mr.at[p], (k, p)).wait_recv()
-
-    @pl.loop(0, S)
-    def _(s):
-        total = mp[s].astype(F32)
-        for p in peers:
-            total = total + mr[p, s].astype(F32)
-        mt[s] = total.astype(BF)
+    def m_copy(s, p, j):
+        return rc(mp.at[s], mr.at[f, s], s_ms.at[s, j], s_mr.at[f, s], (k, p))
+
+    @pl.loop(0, S - 1 - k)
+    def _(i):
+        s = S - 1 - i
+        mp[s] = dot(wout_ref[...], wall[s], 1, 0).astype(BF)
+        for j, p in enumerate(peers):
+            m_copy(s, p, j).start()
 
     far_copy.wait_recv()
     gate(pl.ds(n, n), farr[...].astype(F32))
@@ -203,6 +227,11 @@
 
     for j, p in enumerate(peers):
         h_copy(p, j).start()
+
+    for j in range(1, F - 1):
+        p = peers[j]
+        g_pass(j).wait_recv()
+        g_pass(j).start()
 
     def gp_copy(to):
         return rc(gp.at[k], gp.at[k], s_gps.at[to], s_gpr.at[k], (to, f))
@@ -231,8 +260,13 @@
     @pl.loop(0, S - 1 - k)
     def _(i):
         s = S - 1 - i
+        total = mp[s].astype(F32)
+        for p in peers:
+            rc(mr.at[p, s], mr.at[p, s], s_ms.at[s, 0], s_mr.at[p, s], (k, p)).wait_recv()
+            total = total + mr[p, s].astype(F32)
+        mt[...] = total.astype(BF)
         gp_arrived(s)
-        acc[...] += dot(gp[s], mt[s], 1, 1)
+        acc[...] += dot(gp[s], mt[...], 1, 1)
 
         @pl.when(s == k + 1)
         def _():
@@ -285,7 +319,16 @@
     def _(j):
         p = lax.rem(f + j, F)
         rc(hid.at[p], hid.at[p], s_hs.at[0], s_hr.at[p], (k, p)).wait_recv()
-        rc(gs.at[p], gs.at[p], s_gs.at[0], s_gr.at[p], (k, p)).wait_recv()
+
+        @pl.when(p == sib)
+        def _():
+            rc(
+                gs.at[p, rows(y)], gs.at[p, rows(y)], s_gs.at[0], s_gr.at[y, p], (k, p)
+            ).wait_recv()
+
+        rc(
+            gs.at[p, rows(1 - y)], gs.at[p, rows(1 - y)], s_gs.at[0], s_gr.at[1 - y, p], (k, p)
+        ).wait_recv()
         gout_ref[...] += dot(hid[p], gs[p], 0, 0)
 
     @pl.loop(0, S - 1 - k)
@@ -303,14 +346,22 @@
     for j, p in enumerate(peers):
         for c in x_copies(p, j):
             c.wait_send()
-        for c in (wo_copy, m_copy, pp_copy, g_copy, h_copy, d_copy, u_copy):
+        for c in (pp_copy, g_copy, h_copy, d_copy, u_copy):
             c(p, j).wait_send()
+    g_sib.wait_send()
+    for j in [0] + same:
+        wo_copy(peers[j], j).wait_send()
+    for j in same:
+        wo_pass(j).wait_send()
+    for j in range(1, F - 1):
+        g_pass(j).wait_send()
 
     @pl.loop(0, S - 1 - k)
     def _(i):
         s = S - 1 - i
         for j, p in enumerate(peers):
             c_copy(s, p, j).wait_send()
+            m_copy(s, p, j).wait_send()
 
     far_copy.wait_send()
     e_copy.wait_send()
@@ -404,7 +455,7 @@
             vm((F, 2, n, R), BF),
             vm((S, R, R), BF),
             vm((F, S, R, R), BF),
-            vm((S, R, R), BF),
+            vm((R, R), BF),
             vm((n, R), BF),
             vm((n, R), BF),
             vm((S, 2 * n, R), BF),
@@ -419,11 +470,11 @@
             vm((2 * n, R), F32),
             dma((4,)),
             dma((2, F)), dma((2, F)),
+            dma((F,)), dma((F,)), dma((F,)),
+            dma((S, 3)), dma((S,)),
+            dma((F,)), dma((F,)), dma((2, F)),
             dma((F,)), dma((F,)),
-            dma((S, 3)), dma((S,)),
-            dma((F,)), dma((F,)),
-            dma((F,)), dma((F,)),
-            dma((F,)), dma((F,)),
+            dma((S, F)), dma((F, S)),
             dma((2,)),
             dma((S,)), dma((S,)),
             dma((F,)), dma((F,)),

time: 162 us -> 145 us (0.90)
  Pallas kernels: 151 us -> 136 us
    pallas_call x1, Pallas kernels: 151 us -> 136 us  [on_device(): pl.pallas_call(functools.partial(kernel, S, F), out_shape=(jax.ShapeDtype...]
where the time goes in v3:
time: 145 us
  Pallas kernels  136 us (94%)
  local copies, waits for them, and re-layouts  4.49 us (3%)
  other arithmetic  4.28 us (3%)
    pallas_call x1, Pallas kernels, on_device(): pl.pallas_call(functools.partial(kernel, S, F), out_shape=(jax.ShapeDtype...  136 us
    unnamed x4, local copies, waits for them, and re-layouts  3.32 us

profile of v3, /device:TPU:8, one launch (start us, length us, event | category | flops | bytes accessed | tf_op | source)
XLA Modules:
  0.0 145.3 jit_solution(4751970445274997469)
XLA Ops:
  0.7 0.7 broadcast_multiply_fusion
  1.3 0.8 iota_compare_fusion.1
  2.1 0.1 broadcast_in_dim.79
  2.2 0.1 mul.28
  2.3 0.8 select_reduce_fusion
  3.1 0.1 copy.21
  3.2 1.2 select_reduce_fusion.1
  4.3 0.1 copy.20
  4.4 0.1 broadcast_add_fusion
  4.5 0.1 select_reduce_fusion.2
  4.6 0.1 copy.22
  4.7 0.7 fusion.order_ref
  5.4 0.7 reshape.72.roww_ref
  6.1 135.8 %shard_map.104 = (f32[2048,128]{1,0:T(8,128)}, f32[128,2048]{1,0:T(8,128)}) custom-call(bf16[96,8192]{1,0:T(8,128)(2,1)} %bitcast.9, bf16[96,8192]{1,0:T(8,128)(2,1)} %bitcast.10, bf16[2048,128]{1,0:T(8,128)(2,1)} %bitcast.13, bf16[128,2048]{1,0:T(8,128)(2,1)} %bitcast.14, bf16[192,8192]{1,0:T(8,128)(2,1)} %bitcast.8, f32[192,1]{1,0:T(8,128)} %reshape.72.roww_ref, ...), custom_call_target="tpu_custom_call" | custom-call | flops 1610612736 | bytes 12582912 | tf_op jit(solution)/shard_map/pallas_call | solution.py:440
  141.9 0.0 copy-start
  141.9 2.4 %copy.26 = f32[1,2048,128]{2,1,0:T(8,128)} copy(f32[1,2048,128]{2,1,0:T(8,128)} %bitcast.12) | data formatting | bytes 2097152
  144.3 0.0 copy-done
  144.3 1.0 copy.27
  (4 shorter events, 0.0 us)
Async XLA Ops:
  141.9 2.4 %copy-start = (f32[128,2048]{1,0:T(8,128)S(1)}, f32[128,2048]{1,0:T(8,128)}, u32[]{:S(2)}) copy-start(f32[128,2048]{1,0:T(8,128)} %get-tuple-element.5) | copy-start | bytes 3145732
